TPU v7x, 32 devices: a whole 2x2x4 slice. The times are simulated.
32 devices in a mesh: parts: 1, ctx: 4 (over z), pb: 4 (over y, x), row: 2 (over core).
Axes of the slice: x: 2, y: 2, z: 4, core: 2. Of those that a mesh axis runs over, the one named last changes fastest.
Arguments:
- queries: bfloat16 [2048, 3072], P(('parts', 'ctx', 'pb', 'row')), may hold values from -10 to 10
- cache_keys: bfloat16 [4096, 192], P(('parts', 'ctx')), may hold values from -10 to 10
- cache_values: bfloat16 [4096, 128], P(('parts', 'ctx')), may hold values from -6 to 6
- span_keys: bfloat16 [2048, 192], P(('parts', 'ctx')), may hold values from -10 to 10
- span_values: bfloat16 [2048, 128], P(('parts', 'ctx')), may hold values from -6 to 6
- pool_keys: float32 [32, 192], replicated, may hold values from 0.2 to 0.6
- pool_values: float32 [32, 128], replicated, may hold values from 0.05 to 0.3
- gate_logits: bfloat16 [2048, 48], P(('parts', 'ctx', 'pb', 'row')), may hold values from -6 to 6
- chosen_blocks: int32 [32, 16], P(('parts', 'ctx', 'pb', 'row')), may hold values from 0 to 95, as said below
- valid_counts: int32 [32], P(('parts', 'ctx', 'pb', 'row')), may hold values from 4 to 16
Outputs:
- mixed: bfloat16 [2048, 2048], P(('parts', 'ctx', 'pb', 'row'))
Inputs may be any that keep to these rules, and one draw needn't show every extreme that they name: `chosen_blocks`: slot 0 of tile t holds the tile's own block 64 + t. Slot s > 0 holds a block of the cache stored by ctx index (c + s) mod (4), where c is the ctx index that holds tile t; the blocks of one tile are distinct. Slots at or beyond the tile's valid count hold blocks too and are ignored.
All inputs are finite; a program needn't handle non-finite values.
Results may differ from a plain program's by a relative error of at most 0.0034.
The roundings to bfloat16 on the way count: a program that leaves them out, or rounds other values in their place, can miss the bound.
Values may be sent and summed in bfloat16 or wider, within the bound.
A program may use at most 64 MiB of HBM per device.

v0:
```python
import math
import jax
import jax.numpy as jnp
from jax import lax
from jax.sharding import PartitionSpec as P

HEADS = 16
CLEN = 32
STRIDE = 16
BLOCK = 64
WINDOW = 256
NEG_FILL = -1e30


def from_behind(value, axis, steps):
    count = lax.axis_size(axis)
    pairs = [(source, (source + steps) % count) for source in range(count)]
    return lax.ppermute(value, axis, pairs)


def pool_blocks(rows, extra, weights, stride):
    joined = jnp.concatenate([rows, extra], axis=0).astype(jnp.float32)
    blocks = rows.shape[0] // stride
    grouped = joined.reshape(blocks + 1, stride, rows.shape[1])
    leading = jnp.sum(grouped[:-1] * weights[None, :stride, :], axis=1)
    trailing = jnp.sum(grouped[1:] * weights[None, stride:, :], axis=1)
    return (leading + trailing).astype(jnp.bfloat16)


def attend(query_rows, keys, values, visible, score_scale):
    scores = jnp.dot(query_rows, keys.T, preferred_element_type=jnp.float32) * score_scale
    scores = jnp.where(visible, scores, NEG_FILL)
    highest = jnp.max(scores, axis=1, keepdims=True)
    exponent = jnp.where(visible, jnp.exp(scores - highest), 0.0)
    weights = exponent.astype(jnp.bfloat16)
    numerator = jnp.dot(weights, values, preferred_element_type=jnp.float32)
    return numerator / jnp.sum(exponent, axis=1, keepdims=True)


def local(
    queries,
    cache_keys,
    cache_values,
    span_keys,
    span_values,
    pool_keys,
    pool_values,
    gate_logits,
    chosen_blocks,
    valid_counts,
):
    owners = lax.axis_size("ctx")
    ctx_place = lax.axis_index("ctx")
    tile_place = lax.axis_index("pb") * lax.axis_size("row") + lax.axis_index("row")
    cache_len, key_width = cache_keys.shape
    value_width = cache_values.shape[1]
    span_len = span_keys.shape[0]
    tokens = queries.shape[0]
    tiles_here = chosen_blocks.shape[0]
    score_scale = 1.0 / math.sqrt(key_width)
    context_start = cache_len * owners
    local_start = tile_place * tokens
    first_pos = context_start + ctx_place * span_len + local_start
    row_count = tokens * HEADS
    query_rows = queries.reshape(row_count, key_width)
    row_pos = first_pos + jnp.arange(row_count, dtype=jnp.int32) // HEADS
    leader = ctx_place == 0
    outgoing = (
        jnp.where(leader, span_keys[:STRIDE], cache_keys[:STRIDE]),
        jnp.where(leader, span_values[:STRIDE], cache_values[:STRIDE]),
        span_keys[:STRIDE],
        span_values[:STRIDE],
    )
    heads_next = from_behind((outgoing[0], outgoing[1], outgoing[2], outgoing[3]), "ctx", -1)
    summary_keys = jnp.concatenate(
        [
            pool_blocks(cache_keys, heads_next[0], pool_keys, STRIDE),
            pool_blocks(span_keys, heads_next[2], pool_keys, STRIDE),
        ],
        axis=0,
    )
    summary_values = jnp.concatenate(
        [
            pool_blocks(cache_values, heads_next[1], pool_values, STRIDE),
            pool_blocks(span_values, heads_next[3], pool_values, STRIDE),
        ],
        axis=0,
    )
    cache_blocks = cache_len // STRIDE
    span_blocks = span_len // STRIDE
    per_ctx = cache_blocks + span_blocks
    first_row = jnp.int32(0)
    running_max = jnp.full((row_count,), NEG_FILL, jnp.float32)
    running_sum = jnp.zeros((row_count,), jnp.float32)
    running_out = jnp.zeros((row_count, value_width), jnp.float32)
    part_keys = lax.all_gather(summary_keys, "ctx", axis=0, tiled=True)
    part_values = lax.all_gather(summary_values, "ctx", axis=0, tiled=True)
    length = part_keys.shape[0]
    for lower_row in range(0, length, 512):
        upper_row = min(lower_row + 512, length)
        block_index = first_row + lower_row + jnp.arange(upper_row - lower_row, dtype=jnp.int32)
        owner_of = block_index // per_ctx
        within = block_index % per_ctx
        block_id = jnp.where(
            within < cache_blocks,
            owner_of * cache_blocks + within,
            owners * cache_blocks + owner_of * span_blocks + within - cache_blocks,
        )
        visible = (block_id * STRIDE + CLEN)[None, :] <= row_pos[:, None] + 1
        scores = (
            jnp.dot(
                query_rows, part_keys[lower_row:upper_row].T, preferred_element_type=jnp.float32
            )
            * score_scale
        )
        scores = jnp.where(visible, scores, NEG_FILL)
        new_max = jnp.maximum(running_max, jnp.max(scores, axis=1))
        exponent = jnp.where(visible, jnp.exp(scores - new_max[:, None]), 0.0)
        fading = jnp.exp(running_max - new_max)
        running_sum = running_sum * fading + jnp.sum(exponent, axis=1)
        running_out = running_out * fading[:, None] + jnp.dot(
            exponent.astype(jnp.bfloat16),
            part_values[lower_row:upper_row],
            preferred_element_type=jnp.float32,
        )
        running_max = new_max
    summary_out = running_out / running_sum[:, None]
    reach = chosen_blocks.shape[1] // owners
    arranged = chosen_blocks.reshape(tiles_here, reach, owners)
    column_of = (jnp.arange(owners, dtype=jnp.int32) - ctx_place) % owners
    requested = jnp.take(arranged, column_of, axis=2)
    wanted = lax.all_to_all(requested, "ctx", split_axis=2, concat_axis=2, tiled=True)
    cache_count = cache_len // BLOCK
    span_count = span_len // BLOCK
    from_cache = (wanted < owners * cache_count)[..., None, None]
    cache_slot = jnp.clip(wanted - ctx_place * cache_count, 0, cache_count - 1)
    span_slot = jnp.clip(wanted - owners * cache_count - ctx_place * span_count, 0, span_count - 1)
    served_keys = jnp.where(
        from_cache,
        cache_keys.reshape(cache_count, BLOCK, key_width)[cache_slot],
        span_keys.reshape(span_count, BLOCK, key_width)[span_slot],
    )
    served_values = jnp.where(
        from_cache,
        cache_values.reshape(cache_count, BLOCK, value_width)[cache_slot],
        span_values.reshape(span_count, BLOCK, value_width)[span_slot],
    )
    fetched_keys, fetched_values = (
        lax.all_to_all(served_keys, "ctx", split_axis=2, concat_axis=2, tiled=True),
        lax.all_to_all(served_values, "ctx", split_axis=2, concat_axis=2, tiled=True),
    )
    last_ctx = ctx_place == owners - 1
    tail_rows = from_behind(
        (
            jnp.where(last_ctx, cache_keys[-WINDOW:], span_keys[-WINDOW:]),
            jnp.where(last_ctx, cache_values[-WINDOW:], span_values[-WINDOW:]),
        ),
        "ctx",
        1,
    )
    reach_keys = jnp.concatenate([tail_rows[0], span_keys], axis=0)
    reach_values = jnp.concatenate([tail_rows[1], span_values], axis=0)
    gate_values = jax.nn.sigmoid(gate_logits.astype(jnp.float32)).reshape(tokens, 3, HEADS)
    offsets = jnp.arange(BLOCK, dtype=jnp.int32)
    near_offsets = jnp.arange(WINDOW + BLOCK, dtype=jnp.int32)
    slot_number = jnp.arange(reach, dtype=jnp.int32)[:, None] * owners + column_of[None, :]
    key_pos = (requested[0][:, :, None] * BLOCK + offsets).reshape(-1)
    usable = jnp.repeat((slot_number < valid_counts[0]).reshape(-1), BLOCK)
    sel_visible = usable[None, :] & (key_pos[None, :] <= row_pos[:, None])
    picked = attend(
        query_rows,
        fetched_keys[0].reshape(-1, key_width),
        fetched_values[0].reshape(-1, value_width),
        sel_visible,
        score_scale,
    )
    begin = local_start + 0
    near_keys = lax.dynamic_slice_in_dim(reach_keys, begin, WINDOW + BLOCK, 0)
    near_values = lax.dynamic_slice_in_dim(reach_values, begin, WINDOW + BLOCK, 0)
    near_pos = context_start + ctx_place * span_len - WINDOW + begin + near_offsets
    near_visible = (near_pos[None, :] <= row_pos[:, None]) & (
        near_pos[None, :] > row_pos[:, None] - WINDOW
    )
    nearby = attend(query_rows, near_keys, near_values, near_visible, score_scale)
    mixed = (
        gate_values[:, 0, :, None] * summary_out.reshape(BLOCK, HEADS, value_width)
        + gate_values[:, 1, :, None] * picked.reshape(BLOCK, HEADS, value_width)
        + gate_values[:, 2, :, None] * nearby.reshape(BLOCK, HEADS, value_width)
    )
    outputs = mixed.reshape(BLOCK, HEADS * value_width).astype(jnp.bfloat16)
    return outputs


def solution(mesh):
    return jax.shard_map(
        local,
        mesh=mesh,
        in_specs=(
            P(("parts", "ctx", "pb", "row"), None),
            P(("parts", "ctx"), None),
            P(("parts", "ctx"), None),
            P(("parts", "ctx"), None),
            P(("parts", "ctx"), None),
            P(),
            P(),
            P(("parts", "ctx", "pb", "row"), None),
            P(("parts", "ctx", "pb", "row"), None),
            P(("parts", "ctx", "pb", "row")),
        ),
        out_specs=P(("parts", "ctx", "pb", "row"), None),
        check_vma=False,
    )
```

profile of v0, /device:TPU:0, one launch (start us, length us, event | category | flops | bytes accessed | tf_op | source)
XLA Modules:
  0.0 91.8 jit_solution(5316688061465802636)
XLA Ops:
  0.0 1.3 %copy.79 = bf16[1024,192]{1,0:T(8,128)(2,1)S(1)} copy(bf16[1024,192]{0,1:T(8,128)(2,1)} %param.11) | data formatting | bytes 786432 | tf_op args[1]
  1.3 1.1 %copy.77 = bf16[512,192]{1,0:T(8,128)(2,1)S(1)} copy(bf16[512,192]{0,1:T(8,128)(2,1)} %param.13) | data formatting | bytes 393216 | tf_op args[3]
  2.4 0.6 slice_select_fusion.2
  3.0 5.1 %collective-permute-start = (bf16[16,192]{1,0:T(8,128)(2,1)}, bf16[16,192]{1,0:T(8,128)(2,1)}, u32[]{:S(2)}, u32[]{:S(2)}) collective-permute-start(bf16[16,192]{1,0:T(8,128)(2,1)} %get-tuple-element.13), channel_id=1, source_target_pairs={{0,24},{8,0},{16,8},{24,16},{1,25},{9,1},{17,9},{25,17},{2,26},{10... | collective-permute-start | bytes 18440 | tf_op jit(solution)/shard_map/ppermute | solution.py:18
  8.0 0.4 collective-permute-start.1
  8.5 1.3 %slice_select_fusion.3 = (bf16[16,128]{1,0:T(8,128)(2,1)}, bf16[16,128]{1,0:T(8,128)(2,1)}) fusion(bf16[1024,128]{1,0:T(8,128)(2,1)} %param.12, pred[]{:T(512)S(6)} %eq.10, bf16[512,128]{1,0:T(8,128)(2,1)} %param.14), kind=kLoop, calls=%fused_computation.87 | loop fusion | flops 2048 | bytes 16385 | tf_op jit(solution)/shard_map/jit(_where)/select_n | solution.py:70
  9.8 0.4 collective-permute-start.2
  10.3 0.5 broadcast.494
  10.8 1.3 %reduce.3 = s32[16]{0:T(128)S(1)} reduce(s32[1,16]{1,0:T(1,128)} %param.18, s32[]{:T(128)} %broadcast.494), dimensions={0}, to_apply=%param.18.reduce_sub_computation.3 | reduce | bytes 132 | tf_op args[8]
  12.2 0.1 copy.82
  12.3 0.6 gather_fusion
  12.9 0.1 copy.84
  13.0 0.7 copy.85
  13.7 5.3 %all-to-all-start = ((s32[1,4,4]{1,0,2:T(1,128)}), s32[1,4,4]{1,0,2:T(1,128)S(1)}, u32[]{:S(2)}, u32[]{:S(2)}) async-start(s32[1,4,4]{1,0,2:T(1,128)} %copy.85), calls=%async_computation | async-start | bytes 4096 | tf_op jit(solution)/shard_map/all_to_all | solution.py:132
  18.9 1.0 %slice_select_fusion = bf16[256,192]{0,1:T(8,128)(2,1)S(1)} fusion(bf16[512,192]{0,1:T(8,128)(2,1)} %param.13, bf16[1024,192]{0,1:T(8,128)(2,1)} %param.11, pred[]{:T(512)S(6)} %eq.11), kind=kLoop, calls=%fused_computation.60 | loop fusion | flops 49152 | bytes 294913 | tf_op jit(solution)/shard_map/jit(_where)/select_n | solution.py:155
  19.9 2.1 %collective-permute-start.4 = (bf16[256,192]{0,1:T(8,128)(2,1)S(1)}, bf16[256,192]{0,1:T(8,128)(2,1)}, u32[]{:S(2)}, u32[]{:S(2)}) collective-permute-start(bf16[256,192]{0,1:T(8,128)(2,1)S(1)} %slice_select_fusion), channel_id=1, source_target_pairs={{0,8},{8,16},{16,24},{24,0},{1,9},{9,17},{17,25},{25,1},{2,10},{10... | collective-permute-start | bytes 294920 | tf_op jit(solution)/shard_map/ppermute | solution.py:18
  22.0 0.6 multiply_add_fusion
  22.8 0.6 reshape.297
  23.4 0.1 copy.83
  24.4 0.1 lt.66
  24.5 0.6 and.99
  25.2 0.7 copy.76
  25.9 0.7 copy.81
  26.6 0.7 copy.97
  27.3 0.1 copy.89
  27.5 0.1 copy.91
  27.6 0.1 copy.86
  27.7 0.1 copy.87
  27.9 0.6 gather_fusion.1
  28.4 0.6 gather_fusion.3
  29.1 0.6 gather_fusion.2
  29.6 0.6 gather_fusion.4
  30.2 0.1 broadcast_select_fusion
  30.3 0.7 copy.95
  31.1 3.6 %all-to-all-start.2 = ((bf16[1,4,4,64,128]{4,3,1,0,2:T(8,128)(2,1)}), bf16[1,4,4,64,128]{4,3,1,0,2:T(8,128)(2,1)S(1)}, u32[]{:S(2)}, u32[]{:S(2)}) async-start(bf16[1,4,4,64,128]{4,3,1,0,2:T(8,128)(2,1)} %copy.95), calls=%async_computation.2 | async-start | bytes 524288 | tf_op jit(solution)/shard_map/all_to_all | solution.py:150
  34.7 0.9 copy_select_fusion
  35.6 2.0 %collective-permute-start.5 = (bf16[256,128]{1,0:T(8,128)(2,1)S(1)}, bf16[256,128]{1,0:T(8,128)(2,1)}, u32[]{:S(2)}, u32[]{:S(2)}) collective-permute-start(bf16[256,128]{1,0:T(8,128)(2,1)S(1)} %slice_select_fusion.1), channel_id=1, source_target_pairs={{0,8},{8,16},{16,24},{24,0},{1,9},{9,17},{17,25},{25,1},{2,10},{10... | collective-permute-start | bytes 196616 | tf_op jit(solution)/shard_map/ppermute | solution.py:18
  37.6 0.7 maximum_convert_fusion.2
  38.4 0.7 maximum_convert_fusion.3
  39.2 0.2 multiply_reduce_fusion.2
  39.4 0.1 multiply_reduce_fusion.6
  39.6 13.2 %all_gather.7 = bf16[384,128]{1,0:T(8,128)(2,1)S(1)} all-gather(bf16[96,128]{1,0:T(8,128)(2,1)S(1)} %pad_maximum_fusion.1), channel_id=1, replica_groups=mesh['parts'=1,'ctx'=4,'pb'=4,'row'=2] {'ctx'}, dimensions={0}, use_global_device_ids=true | all-gather | bytes 122880 | tf_op jit(solution)/shard_map/all_gather | solution.py:97
  52.8 0.8 maximum_convert_fusion
  53.6 0.2 fusion.53
  53.8 0.7 maximum_convert_fusion.1
  54.6 0.5 multiply_reduce_fusion
  55.2 0.3 multiply_reduce_fusion.4
  55.5 13.6 %all_gather.6 = bf16[384,192]{1,0:T(8,128)(2,1)S(1)} all-gather(bf16[96,192]{1,0:T(8,128)(2,1)S(1)} %pad_maximum_fusion), channel_id=1, replica_groups=mesh['parts'=1,'ctx'=4,'pb'=4,'row'=2] {'ctx'}, dimensions={0}, use_global_device_ids=true | all-gather | bytes 184320 | tf_op jit(solution)/shard_map/all_gather | solution.py:96
  69.0 0.4 fusion.60
  69.5 0.3 fusion.9
  69.8 0.7 fusion.5
  70.6 3.7 %all-to-all-start.1 = ((bf16[1,4,4,64,192]{4,3,1,0,2:T(8,128)(2,1)}), bf16[1,4,4,64,192]{4,3,1,0,2:T(8,128)(2,1)S(1)}, u32[]{:S(2)}, u32[]{:S(2)}) async-start(bf16[1,4,4,64,192]{4,3,1,0,2:T(8,128)(2,1)} %copy_select_fusion), calls=%async_computation.1 | async-start | bytes 1048576 | tf_op jit(solution)/shard_map/all_to_all | solution.py:149
  74.3 1.7 %fusion.59 = (f32[1024]{0:T(1024)S(1)}, f32[1024,320]{0,1:T(8,128)S(1)}) fusion(bf16[1024,192]{1,0:T(8,128)(2,1)S(1)} %reshape.297, s32[]{:T(128)S(6)} %select_n.211, bf16[256,192]{0,1:T(8,128)(2,1)} %collective-permute-done.4, bf16[512,192]{0,1:T(8,128)(2,1)S(1)} %copy-done.2, s32[1024]{0:T(1024)S(1)} %broadcast_add_fusion, s32[1024]{0:T(1024)S(1)} %fusion.31, ...), kind=kOutput, calls=%fused_computation.137 | convolution fusion | flops 128039936 | bytes 2012420 | tf_op jit(solution)/shard_map/dot_general | solution.py:31
  76.0 0.4 fusion.11
  76.4 1.5 %convolution_divide_fusion = f32[1024,128]{1,0:T(8,128)S(1)} fusion(f32[1024,320]{0,1:T(8,128)S(1)} %get-tuple-element.29, f32[1024]{0:T(1024)S(1)} %get-tuple-element.28, s32[1024]{0:T(1024)S(1)} %broadcast_add_fusion, s32[1024]{0:T(1024)S(1)} %fusion.31, s32[320]{0:T(512)S(1)} %iota_add_fusion.1, f32[1024]{0:T(1024)S(1)} %fusion.11, s32[]{:T(128)S(6)} %select_n.211, ...), kind=kOutput, calls=%fused_computation.21 | convolution fusion | flops 86147072 | bytes 2049284 | tf_op jit(solution)/shard_map/dot_general | solution.py:36
  78.0 6.4 %all-to-all-done.1 = bf16[1,4,4,64,192]{4,3,1,0,2:T(8,128)(2,1)S(1)} async-done(((bf16[1,4,4,64,192]{4,3,1,0,2:T(8,128)(2,1)}), bf16[1,4,4,64,192]{4,3,1,0,2:T(8,128)(2,1)S(1)}, u32[]{:S(2)}, u32[]{:S(2)}) %all-to-all-start.1) | async-done | bytes 393248 | tf_op jit(solution)/shard_map/all_to_all | solution.py:149
  84.4 1.2 %fusion = (f32[1024]{0:T(1024)S(1)}, f32[1024,1024]{1,0:T(8,128)S(1)}) fusion(s32[1024]{0:T(1024)S(1)} %fusion.31, s32[1024]{0:T(1024)S(1)} %add.265, pred[1024]{0:T(1024)(128)(4,1)S(1)} %copy-done.11, bf16[1024,192]{1,0:T(8,128)(2,1)S(1)} %bitcast.97, bf16[1024,192]{1,0:T(8,128)(2,1)S(1)} %reshape.297), kind=kOutput, calls=%fused_computation.8 | convolution fusion | flops 407895040 | bytes 4994048 | tf_op jit(solution)/shard_map/dot_general | solution.py:31
  85.6 1.9 %fusion.52 = f32[1024]{0:T(1024)S(1)} fusion(f32[1024]{0:T(1024)S(1)} %get-tuple-element.30, f32[1024,1024]{1,0:T(8,128)S(1)} %get-tuple-element.31, s32[1024]{0:T(1024)S(1)} %fusion.31, s32[1024]{0:T(1024)S(1)} %add.265, pred[1024]{0:T(1024)(128)(4,1)S(1)} %copy-done.11), kind=kLoop, calls=%fused_computation.130 | loop fusion | flops 7339008 | bytes 4211712 | tf_op jit(solution)/shard_map/reduce_sum | solution.py:37
  87.5 1.8 %fusion.6 = f32[1024,128]{1,0:T(8,128)S(1)} fusion(bf16[1024,128]{1,0:T(8,128)(2,1)S(1)} %bitcast.98, f32[1024]{0:T(1024)S(1)} %fusion.52, f32[1024,1024]{1,0:T(8,128)S(1)} %get-tuple-element.31, f32[1024]{0:T(1024)S(1)} %get-tuple-element.30, s32[1024]{0:T(1024)S(1)} %fusion.31, s32[1024]{0:T(1024)S(1)} %add.265, pred[1024]{0:T(1024)(128)(4,1)S(1)} %copy-done.11), kind=kOutput, calls=%fused_computation.20 | convolution fusion | flops 275906560 | bytes 4998144 | tf_op jit(solution)/shard_map/dot_general | solution.py:36
  89.5 0.2 mul.192
  89.7 0.4 copy-done.5
  90.2 0.2 mul.223
  90.4 0.2 mul.234
  90.6 1.3 %fusion.25 = bf16[64,2048]{1,0:T(8,128)(2,1)} fusion(f32[64,2048]{1,0:T(8,128)S(1)} %reshape.305, f32[8,8,16,128]{3,2,1,0:T(8,128)S(1)} %bitcast.92, f32[64,2048]{1,0:T(8,128)S(1)} %reshape.304, f32[8,8,16,128]{3,2,1,0:T(8,128)S(1)} %bitcast.91, f32[64,2048]{1,0:T(8,128)S(1)} %reshape.298, f32[8,8,16,128]{3,2,1,0:T(8,128)S(1)} %bitcast.90), kind=kLoop, calls=%fused_computation.40 | loop fusion | flops 786432 | bytes 3407872 | tf_op jit(solution)/shard_map/convert_element_type | solution.py:190
  (75 shorter events, 1.4 us)
Async XLA Ops:
  0.0 22.7 %copy-start.1 = (bf16[1024,128]{1,0:T(8,128)(2,1)S(1)}, bf16[1024,128]{1,0:T(8,128)(2,1)}, u32[]{:S(2)}) copy-start(bf16[1024,128]{1,0:T(8,128)(2,1)} %param.12) | copy-start | bytes 786436
  0.0 22.7 %copy-start = (bf16[512,128]{1,0:T(8,128)(2,1)S(1)}, bf16[512,128]{1,0:T(8,128)(2,1)}, u32[]{:S(2)}) copy-start(bf16[512,128]{1,0:T(8,128)(2,1)} %param.14) | copy-start | bytes 393220
  0.0 22.7 %copy-start.7 = (f32[32,192]{1,0:T(8,128)S(1)}, f32[32,192]{1,0:T(8,128)}, u32[]{:S(2)}) copy-start(f32[32,192]{1,0:T(8,128)} %param.15) | copy-start | bytes 73732
  0.0 22.7 %copy-start.3 = (bf16[64,3072]{1,0:T(8,128)(2,1)S(1)}, bf16[64,3072]{1,0:T(8,128)(2,1)}, u32[]{:S(2)}) copy-start(bf16[64,3072]{1,0:T(8,128)(2,1)} %param.10) | copy-start | bytes 1179652
  0.0 23.4 %copy-start.8 = (f32[32,128]{1,0:T(8,128)S(1)}, f32[32,128]{1,0:T(8,128)}, u32[]{:S(2)}) copy-start(f32[32,128]{1,0:T(8,128)} %param.16) | copy-start | bytes 49156
  0.0 25.2 %copy-start.9 = (bf16[64,48]{0,1:T(8,128)(2,1)S(1)}, bf16[64,48]{0,1:T(8,128)(2,1)}, u32[]{:S(2)}) copy-start(bf16[64,48]{0,1:T(8,128)(2,1)} %param.17) | copy-start | bytes 18436
  3.0 49.8 %collective-permute-start = (bf16[16,192]{1,0:T(8,128)(2,1)}, bf16[16,192]{1,0:T(8,128)(2,1)}, u32[]{:S(2)}, u32[]{:S(2)}) collective-permute-start(bf16[16,192]{1,0:T(8,128)(2,1)} %get-tuple-element.13), channel_id=1, source_target_pairs={{0,24},{8,0},{16,8},{24,16},{1,25},{9,1},{17,9},{25,17},{2,26},{10... | collective-permute-start | bytes 18440 | tf_op jit(solution)/shard_map/ppermute | solution.py:18
  8.0 45.7 %collective-permute-start.1 = (bf16[16,192]{1,0:T(8,128)(2,1)}, bf16[16,192]{1,0:T(8,128)(2,1)}, u32[]{:S(2)}, u32[]{:S(2)}) collective-permute-start(bf16[16,192]{1,0:T(8,128)(2,1)} %get-tuple-element.14), channel_id=1, source_target_pairs={{0,24},{8,0},{16,8},{24,16},{1,25},{9,1},{17,9},{25,17},{2,26},{10... | collective-permute-start | bytes 18440 | tf_op jit(solution)/shard_map/ppermute | solution.py:18
  9.8 25.8 %collective-permute-start.2 = (bf16[16,128]{1,0:T(8,128)(2,1)}, bf16[16,128]{1,0:T(8,128)(2,1)}, u32[]{:S(2)}, u32[]{:S(2)}) collective-permute-start(bf16[16,128]{1,0:T(8,128)(2,1)} %get-tuple-element.15), channel_id=1, source_target_pairs={{0,24},{8,0},{16,8},{24,16},{1,25},{9,1},{17,9},{25,17},{2,26},{10... | collective-permute-start | bytes 12296 | tf_op jit(solution)/shard_map/ppermute | solution.py:18
  10.2 28.2 %collective-permute-start.3 = (bf16[16,128]{1,0:T(8,128)(2,1)}, bf16[16,128]{1,0:T(8,128)(2,1)}, u32[]{:S(2)}, u32[]{:S(2)}) collective-permute-start(bf16[16,128]{1,0:T(8,128)(2,1)} %get-tuple-element.16), channel_id=1, source_target_pairs={{0,24},{8,0},{16,8},{24,16},{1,25},{9,1},{17,9},{25,17},{2,26},{10... | collective-permute-start | bytes 12296 | tf_op jit(solution)/shard_map/ppermute | solution.py:18
  13.7 13.6 %all-to-all-start = ((s32[1,4,4]{1,0,2:T(1,128)}), s32[1,4,4]{1,0,2:T(1,128)S(1)}, u32[]{:S(2)}, u32[]{:S(2)}) async-start(s32[1,4,4]{1,0,2:T(1,128)} %copy.85), calls=%async_computation | async-start | bytes 4096 | tf_op jit(solution)/shard_map/all_to_all | solution.py:132
  19.9 54.4 %collective-permute-start.4 = (bf16[256,192]{0,1:T(8,128)(2,1)S(1)}, bf16[256,192]{0,1:T(8,128)(2,1)}, u32[]{:S(2)}, u32[]{:S(2)}) collective-permute-start(bf16[256,192]{0,1:T(8,128)(2,1)S(1)} %slice_select_fusion), channel_id=1, source_target_pairs={{0,8},{8,16},{16,24},{24,0},{1,9},{9,17},{17,25},{25,1},{2,10},{10... | collective-permute-start | bytes 294920 | tf_op jit(solution)/shard_map/ppermute | solution.py:18
  31.1 39.6 %all-to-all-start.2 = ((bf16[1,4,4,64,128]{4,3,1,0,2:T(8,128)(2,1)}), bf16[1,4,4,64,128]{4,3,1,0,2:T(8,128)(2,1)S(1)}, u32[]{:S(2)}, u32[]{:S(2)}) async-start(bf16[1,4,4,64,128]{4,3,1,0,2:T(8,128)(2,1)} %copy.95), calls=%async_computation.2 | async-start | bytes 524288 | tf_op jit(solution)/shard_map/all_to_all | solution.py:150
  35.6 40.8 %collective-permute-start.5 = (bf16[256,128]{1,0:T(8,128)(2,1)S(1)}, bf16[256,128]{1,0:T(8,128)(2,1)}, u32[]{:S(2)}, u32[]{:S(2)}) collective-permute-start(bf16[256,128]{1,0:T(8,128)(2,1)S(1)} %slice_select_fusion.1), channel_id=1, source_target_pairs={{0,8},{8,16},{16,24},{24,0},{1,9},{9,17},{17,25},{25,1},{2,10},{10... | collective-permute-start | bytes 196616 | tf_op jit(solution)/shard_map/ppermute | solution.py:18
  54.6 14.4 %copy-start.10 = (s32[384]{0:T(512)S(1)}, s32[384]{0:T(512)}, u32[]{:S(2)}) copy-start(s32[384]{0:T(512)} %multiply_add_fusion) | copy-start | bytes 4612
  70.5 3.8 %copy-start.2 = (bf16[512,192]{0,1:T(8,128)(2,1)S(1)}, bf16[512,192]{0,1:T(8,128)(2,1)}, u32[]{:S(2)}) copy-start(bf16[512,192]{0,1:T(8,128)(2,1)} %param.13) | copy-start | bytes 589828
  70.6 13.7 %all-to-all-start.1 = ((bf16[1,4,4,64,192]{4,3,1,0,2:T(8,128)(2,1)}), bf16[1,4,4,64,192]{4,3,1,0,2:T(8,128)(2,1)S(1)}, u32[]{:S(2)}, u32[]{:S(2)}) async-start(bf16[1,4,4,64,192]{4,3,1,0,2:T(8,128)(2,1)} %copy_select_fusion), calls=%async_computation.1 | async-start | bytes 1048576 | tf_op jit(solution)/shard_map/all_to_all | solution.py:149
  77.9 6.5 %copy-start.11 = (pred[1024]{0:T(1024)(128)(4,1)S(1)}, pred[1024]{0:T(1024)(128)(4,1)}, u32[]{:S(2)}) copy-start(pred[1024]{0:T(1024)(128)(4,1)} %and.99) | copy-start | bytes 3076
  87.5 2.0 %copy-start.4 = (f32[64,16]{1,0:T(8,128)S(1)}, f32[64,16]{1,0:T(8,128)}, u32[]{:S(2)}) copy-start(f32[64,16]{1,0:T(8,128)} %copy.76) | copy-start | bytes 12292
  89.4 0.8 copy-start.5
  89.4 0.9 %copy-start.6 = (f32[64,16]{1,0:T(8,128)S(1)}, f32[64,16]{1,0:T(8,128)}, u32[]{:S(2)}) copy-start(f32[64,16]{1,0:T(8,128)} %copy.97) | copy-start | bytes 12292
where the time goes:
time: 92.6 us; the launch traced here: 91.8 us
  blocking collectives  26.8 us (29%)
  starting transfers between devices  22.7 us (25%)
  other arithmetic  14.1 us (15%)
  local copies, waits for them, and re-layouts  13.3 us (14%)
  matrix products  7.31 us (8%)
  waiting for transfers between devices  6.38 us (7%)
  between operations  1.25 us (1%)
    all_gather x1, blocking collectives, local(): part_keys = lax.all_gather(summary_keys, 'ctx', axis=0, tiled=True)  13.6 us
    all_gather x1, blocking collectives, local(): part_values = lax.all_gather(summary_values, 'ctx', axis=0, tiled=True)  13.2 us
    ppermute x6, starting transfers between devices, from_behind(): return lax.ppermute(value, axis, pairs)  10.1 us
    all_to_all x1, waiting for transfers between devices, local(): lax.all_to_all(served_keys, 'ctx', split_axis=2, concat_axis=2, tiled=True)  6.36 us
    all_to_all x1, starting transfers between devices, local(): lax.all_to_all(requested, 'ctx', split_axis=2, concat_axis=2, tiled=True)  5.27 us
    all_to_all x1, starting transfers between devices, local(): lax.all_to_all(served_keys, 'ctx', split_axis=2, concat_axis=2, tiled=True)  3.66 us
    all_to_all x1, starting transfers between devices, local(): lax.all_to_all(served_values, 'ctx', split_axis=2, concat_axis=2, tiled=T...  3.63 us
    unnamed x27, local copies, waits for them, and re-layouts  3.33 us
  transfers between devices with their start and end apart: 9, of which 1 were waited for; matrix products, arithmetic and copies ran while one was open for 27% of the time, Pallas kernels for 0%

commit v1 on v0

--- a/solution.py
+++ b/solution.py
@@ -94,7 +94,16 @@
     running_sum = jnp.zeros((row_count,), jnp.float32)
     running_out = jnp.zeros((row_count, value_width), jnp.float32)
     part_keys = lax.all_gather(summary_keys, "ctx", axis=0, tiled=True)
-    part_values = lax.all_gather(summary_values, "ctx", axis=0, tiled=True)
+    t1 = jax.lax.axis_size("ctx")
+    before, z = (t1, jax.lax.axis_index("ctx"))
+    part_values, z_new = (summary_values, 1)
+    while z_new < before:
+        w_next = tuple(((nth, nth ^ z_new) for nth in range(before)))
+        earlier = jax.lax.ppermute(part_values, axis_name="ctx", perm=w_next)
+        everything = jnp.concatenate([part_values, earlier], axis=0)
+        shaped = jnp.concatenate([earlier, part_values], axis=0)
+        part_values = jnp.where(z & z_new == 0, everything, shaped)
+        z_new = 2 * z_new
     length = part_keys.shape[0]
     for lower_row in range(0, length, 512):
         upper_row = min(lower_row + 512, length)

time: 92.6 us -> 87.1 us (0.941)
  blocking collectives: 26.8 us -> 13.6 us
  waiting for transfers between devices: 6.38 us -> 11.2 us
  starting transfers between devices: 22.7 us -> 24.9 us
    all_gather x1 -> x0, blocking collectives: 13.2 us -> none  [local(): part_values = lax.all_gather(summary_values, 'ctx', axis=0, tiled=True)]
    ppermute x0 -> x2, waiting for transfers between devices: none -> 4.88 us  [local(): earlier = jax.lax.ppermute(part_values, axis_name='ctx', perm=w_next)]
    ppermute x0 -> x2, starting transfers between devices: none -> 2.22 us  [local(): earlier = jax.lax.ppermute(part_values, axis_name='ctx', perm=w_next)]
    unnamed x27 -> x29, local copies, waits for them, and re-layouts: 3.33 us -> 3.33 us
  transfers between devices with their start and end apart: 9 -> 11, of which waited for: 1 -> 2; matrix products, arithmetic and copies ran while one was open for 27% -> 29% of each run, Pallas kernels for 0% -> 0%
where the time goes in v1:
time: 87.1 us; the launch traced here: 86.4 us
  starting transfers between devices  24.9 us (29%)
  other arithmetic  14.7 us (17%)
  blocking collectives  13.6 us (16%)
  local copies, waits for them, and re-layouts  13.4 us (15%)
  waiting for transfers between devices  11.2 us (13%)
  matrix products  7.33 us (8%)
  between operations  1.28 us (1%)
    all_gather x1, blocking collectives, local(): part_keys = lax.all_gather(summary_keys, 'ctx', axis=0, tiled=True)  13.6 us
    ppermute x6, starting transfers between devices, from_behind(): return lax.ppermute(value, axis, pairs)  10.1 us
    all_to_all x1, waiting for transfers between devices, local(): lax.all_to_all(served_keys, 'ctx', split_axis=2, concat_axis=2, tiled=True)  6.34 us
    all_to_all x1, starting transfers between devices, local(): lax.all_to_all(requested, 'ctx', split_axis=2, concat_axis=2, tiled=True)  5.27 us
    ppermute x2, waiting for transfers between devices, local(): earlier = jax.lax.ppermute(part_values, axis_name='ctx', perm=w_next)  4.88 us
    all_to_all x1, starting transfers between devices, local(): lax.all_to_all(served_keys, 'ctx', split_axis=2, concat_axis=2, tiled=True)  3.66 us
    all_to_all x1, starting transfers between devices, local(): lax.all_to_all(served_values, 'ctx', split_axis=2, concat_axis=2, tiled=T...  3.63 us
    unnamed x29, local copies, waits for them, and re-layouts  3.33 us
  transfers between devices with their start and end apart: 11, of which 2 were waited for; matrix products, arithmetic and copies ran while one was open for 29% of the time, Pallas kernels for 0%

profile of v1, /device:TPU:0, one launch (start us, length us, event | category | flops | bytes accessed | tf_op | source)
XLA Modules:
  0.0 86.4 jit_solution(10716105018812927314)
XLA Ops:
  0.0 1.3 %copy.79 = bf16[1024,192]{1,0:T(8,128)(2,1)S(1)} copy(bf16[1024,192]{0,1:T(8,128)(2,1)} %param.11) | data formatting | bytes 786432 | tf_op args[1]
  1.3 1.1 %copy.77 = bf16[512,192]{1,0:T(8,128)(2,1)S(1)} copy(bf16[512,192]{0,1:T(8,128)(2,1)} %param.13) | data formatting | bytes 393216 | tf_op args[3]
  2.4 0.6 slice_select_fusion.2
  3.0 5.1 %collective-permute-start = (bf16[16,192]{1,0:T(8,128)(2,1)}, bf16[16,192]{1,0:T(8,128)(2,1)}, u32[]{:S(2)}, u32[]{:S(2)}) collective-permute-start(bf16[16,192]{1,0:T(8,128)(2,1)} %get-tuple-element.13), channel_id=1, source_target_pairs={{0,24},{8,0},{16,8},{24,16},{1,25},{9,1},{17,9},{25,17},{2,26},{10... | collective-permute-start | bytes 18440 | tf_op jit(solution)/shard_map/ppermute | solution.py:18
  8.0 0.4 collective-permute-start.1
  8.5 1.3 %slice_select_fusion.3 = (bf16[16,128]{1,0:T(8,128)(2,1)}, bf16[16,128]{1,0:T(8,128)(2,1)}) fusion(bf16[1024,128]{1,0:T(8,128)(2,1)} %param.12, pred[]{:T(512)S(6)} %eq.16, bf16[512,128]{1,0:T(8,128)(2,1)} %param.14), kind=kLoop, calls=%fused_computation.95 | loop fusion | flops 2048 | bytes 16385 | tf_op jit(solution)/shard_map/jit(_where)/select_n | solution.py:70
  9.8 0.4 collective-permute-start.2
  10.3 0.5 broadcast.494
  10.8 1.3 %reduce.3 = s32[16]{0:T(128)S(1)} reduce(s32[1,16]{1,0:T(1,128)} %param.18, s32[]{:T(128)} %broadcast.494), dimensions={0}, to_apply=%param.18.reduce_sub_computation.3 | reduce | bytes 132 | tf_op args[8]
  12.3 0.1 copy.82
  12.3 0.6 gather_fusion
  12.9 0.1 copy.84
  13.0 0.7 copy.85
  13.7 5.3 %all-to-all-start = ((s32[1,4,4]{1,0,2:T(1,128)}), s32[1,4,4]{1,0,2:T(1,128)S(1)}, u32[]{:S(2)}, u32[]{:S(2)}) async-start(s32[1,4,4]{1,0,2:T(1,128)} %copy.85), calls=%async_computation | async-start | bytes 4096 | tf_op jit(solution)/shard_map/all_to_all | solution.py:141
  18.9 1.0 %slice_select_fusion = bf16[256,192]{0,1:T(8,128)(2,1)S(1)} fusion(bf16[512,192]{0,1:T(8,128)(2,1)} %param.13, bf16[1024,192]{0,1:T(8,128)(2,1)} %param.11, pred[]{:T(512)S(6)} %eq.19), kind=kLoop, calls=%fused_computation.66 | loop fusion | flops 49152 | bytes 294913 | tf_op jit(solution)/shard_map/jit(_where)/select_n | solution.py:164
  19.9 2.1 %collective-permute-start.6 = (bf16[256,192]{0,1:T(8,128)(2,1)S(1)}, bf16[256,192]{0,1:T(8,128)(2,1)}, u32[]{:S(2)}, u32[]{:S(2)}) collective-permute-start(bf16[256,192]{0,1:T(8,128)(2,1)S(1)} %slice_select_fusion), channel_id=1, source_target_pairs={{0,8},{8,16},{16,24},{24,0},{1,9},{9,17},{17,25},{25,1},{2,10},{10... | collective-permute-start | bytes 294920 | tf_op jit(solution)/shard_map/ppermute | solution.py:18
  22.0 0.6 multiply_add_fusion
  22.8 0.6 reshape.297
  23.4 0.1 copy.83
  24.5 0.7 and.107
  25.2 0.6 iota_add_fusion.1
  25.8 0.7 copy.76
  26.5 0.7 copy.81
  27.2 0.7 copy.97
  27.9 0.1 copy.89
  28.1 0.1 copy.91
  28.4 0.1 copy.87
  28.5 0.6 gather_fusion.1
  29.1 0.6 gather_fusion.3
  29.7 0.6 gather_fusion.2
  30.3 0.6 gather_fusion.4
  31.0 0.7 copy.95
  31.7 3.6 %all-to-all-start.2 = ((bf16[1,4,4,64,128]{4,3,1,0,2:T(8,128)(2,1)}), bf16[1,4,4,64,128]{4,3,1,0,2:T(8,128)(2,1)S(1)}, u32[]{:S(2)}, u32[]{:S(2)}) async-start(bf16[1,4,4,64,128]{4,3,1,0,2:T(8,128)(2,1)} %copy.95), calls=%async_computation.2 | async-start | bytes 524288 | tf_op jit(solution)/shard_map/all_to_all | solution.py:159
  35.4 0.9 %copy_select_fusion = bf16[1,4,4,64,192]{4,3,1,0,2:T(8,128)(2,1)} fusion(bf16[1,4,4,64,192]{4,3,2,1,0:T(8,128)(2,1)S(1)} %bitcast.88, bf16[1,4,4,64,192]{4,3,2,1,0:T(8,128)(2,1)S(1)} %bitcast.87, pred[4,4]{0,1:T(4,128)(4,1)S(1)} %copy.87), kind=kLoop, calls=%fused_computation.44 | loop fusion | flops 196608 | bytes 1179664 | tf_op jit(solution)/shard_map/jit(_where)/select_n | solution.py:147
  36.3 2.0 %collective-permute-start.7 = (bf16[256,128]{1,0:T(8,128)(2,1)S(1)}, bf16[256,128]{1,0:T(8,128)(2,1)}, u32[]{:S(2)}, u32[]{:S(2)}) collective-permute-start(bf16[256,128]{1,0:T(8,128)(2,1)S(1)} %slice_select_fusion.1), channel_id=1, source_target_pairs={{0,8},{8,16},{16,24},{24,0},{1,9},{9,17},{17,25},{25,1},{2,10},{10... | collective-permute-start | bytes 196616 | tf_op jit(solution)/shard_map/ppermute | solution.py:18
  38.3 0.7 maximum_convert_fusion.2
  39.1 0.7 maximum_convert_fusion.3
  39.8 0.2 multiply_reduce_fusion.2
  40.1 0.1 multiply_reduce_fusion.6
  40.2 1.5 %collective-permute-start.4 = (bf16[96,128]{1,0:T(8,128)(2,1)S(1)}, bf16[96,128]{1,0:T(8,128)(2,1)S(1)}, u32[]{:S(2)}, u32[]{:S(2)}) collective-permute-start(bf16[96,128]{1,0:T(8,128)(2,1)S(1)} %pad_maximum_fusion.1), channel_id=1, source_target_pairs={{0,8},{8,0},{16,24},{24,16},{1,9},{9,1},{17,25},{25,17},{2,10},{10... | collective-permute-start | bytes 73736 | tf_op jit(solution)/shard_map/ppermute | solution.py:102
  41.8 0.8 maximum_convert_fusion
  42.5 0.2 fusion.60
  42.7 0.7 maximum_convert_fusion.1
  43.5 0.5 multiply_reduce_fusion
  44.1 0.3 multiply_reduce_fusion.4
  44.4 13.6 %all_gather.3 = bf16[384,192]{1,0:T(8,128)(2,1)S(1)} all-gather(bf16[96,192]{1,0:T(8,128)(2,1)S(1)} %pad_maximum_fusion), channel_id=1, replica_groups=mesh['parts'=1,'ctx'=4,'pb'=4,'row'=2] {'ctx'}, dimensions={0}, use_global_device_ids=true | all-gather | bytes 184320 | tf_op jit(solution)/shard_map/all_gather | solution.py:96
  58.0 0.4 fusion.67
  58.4 0.3 fusion.9
  58.8 0.7 collective-permute-start.5
  59.5 4.9 %collective-permute-done.5 = bf16[192,128]{1,0:T(8,128)(2,1)S(1)} collective-permute-done((bf16[192,128]{1,0:T(8,128)(2,1)S(1)}, bf16[192,128]{1,0:T(8,128)(2,1)S(1)}, u32[]{:S(2)}, u32[]{:S(2)}) %collective-permute-start.5) | collective-permute-done | bytes 49184 | tf_op jit(solution)/shard_map/ppermute | solution.py:102
  64.4 0.7 fusion.5
  65.2 3.7 %all-to-all-start.1 = ((bf16[1,4,4,64,192]{4,3,1,0,2:T(8,128)(2,1)}), bf16[1,4,4,64,192]{4,3,1,0,2:T(8,128)(2,1)S(1)}, u32[]{:S(2)}, u32[]{:S(2)}) async-start(bf16[1,4,4,64,192]{4,3,1,0,2:T(8,128)(2,1)} %copy_select_fusion), calls=%async_computation.1 | async-start | bytes 1048576 | tf_op jit(solution)/shard_map/all_to_all | solution.py:158
  68.9 1.7 %fusion.66 = (f32[1024]{0:T(1024)S(1)}, f32[1024,320]{0,1:T(8,128)S(1)}) fusion(bf16[1024,192]{1,0:T(8,128)(2,1)S(1)} %reshape.297, s32[]{:T(128)S(6)} %select_n.231, bf16[256,192]{0,1:T(8,128)(2,1)} %collective-permute-done.6, bf16[512,192]{0,1:T(8,128)(2,1)S(1)} %copy-done.2, s32[1024]{0:T(1024)S(1)} %broadcast_add_fusion, s32[1024]{0:T(1024)S(1)} %fusion.37, ...), kind=kOutput, calls=%fused_computation.146 | convolution fusion | flops 128039936 | bytes 2012420 | tf_op jit(solution)/shard_map/dot_general | solution.py:31
  70.6 0.4 fusion.11
  71.0 1.5 %convolution_divide_fusion = f32[1024,128]{1,0:T(8,128)S(1)} fusion(f32[1024,320]{0,1:T(8,128)S(1)} %get-tuple-element.29, f32[1024]{0:T(1024)S(1)} %get-tuple-element.28, s32[1024]{0:T(1024)S(1)} %broadcast_add_fusion, s32[1024]{0:T(1024)S(1)} %fusion.37, s32[320]{0:T(512)S(1)} %copy-done.10, f32[1024]{0:T(1024)S(1)} %fusion.11, s32[]{:T(128)S(6)} %select_n.231, ...), kind=kOutput, calls=%fused_computation.21 | convolution fusion | flops 86147072 | bytes 2049284 | tf_op jit(solution)/shard_map/dot_general | solution.py:36
  72.6 6.3 %all-to-all-done.1 = bf16[1,4,4,64,192]{4,3,1,0,2:T(8,128)(2,1)S(1)} async-done(((bf16[1,4,4,64,192]{4,3,1,0,2:T(8,128)(2,1)}), bf16[1,4,4,64,192]{4,3,1,0,2:T(8,128)(2,1)S(1)}, u32[]{:S(2)}, u32[]{:S(2)}) %all-to-all-start.1) | async-done | bytes 393248 | tf_op jit(solution)/shard_map/all_to_all | solution.py:158
  79.0 1.2 %fusion = (f32[1024]{0:T(1024)S(1)}, f32[1024,1024]{1,0:T(8,128)S(1)}) fusion(s32[1024]{0:T(1024)S(1)} %fusion.37, s32[1024]{0:T(1024)S(1)} %add.265, pred[1024]{0:T(1024)(128)(4,1)S(1)} %copy-done.12, bf16[1024,192]{1,0:T(8,128)(2,1)S(1)} %bitcast.96, bf16[1024,192]{1,0:T(8,128)(2,1)S(1)} %reshape.297), kind=kOutput, calls=%fused_computation.8 | convolution fusion | flops 407895040 | bytes 4994048 | tf_op jit(solution)/shard_map/dot_general | solution.py:31
  80.2 1.9 %fusion.59 = f32[1024]{0:T(1024)S(1)} fusion(f32[1024]{0:T(1024)S(1)} %get-tuple-element.30, f32[1024,1024]{1,0:T(8,128)S(1)} %get-tuple-element.31, s32[1024]{0:T(1024)S(1)} %fusion.37, s32[1024]{0:T(1024)S(1)} %add.265, pred[1024]{0:T(1024)(128)(4,1)S(1)} %copy-done.12), kind=kLoop, calls=%fused_computation.139 | loop fusion | flops 7339008 | bytes 4211712 | tf_op jit(solution)/shard_map/reduce_sum | solution.py:37
  82.1 1.8 %fusion.6 = f32[1024,128]{1,0:T(8,128)S(1)} fusion(bf16[1024,128]{1,0:T(8,128)(2,1)S(1)} %bitcast.97, f32[1024]{0:T(1024)S(1)} %fusion.59, f32[1024,1024]{1,0:T(8,128)S(1)} %get-tuple-element.31, f32[1024]{0:T(1024)S(1)} %get-tuple-element.30, s32[1024]{0:T(1024)S(1)} %fusion.37, s32[1024]{0:T(1024)S(1)} %add.265, pred[1024]{0:T(1024)(128)(4,1)S(1)} %copy-done.12), kind=kOutput, calls=%fused_computation.20 | convolution fusion | flops 275906560 | bytes 4998144 | tf_op jit(solution)/shard_map/dot_general | solution.py:36
  84.1 0.2 mul.192
  84.3 0.4 copy-done.5
  84.7 0.2 mul.223
  84.9 0.2 mul.234
  85.1 1.3 %fusion.25 = bf16[64,2048]{1,0:T(8,128)(2,1)} fusion(f32[64,2048]{1,0:T(8,128)S(1)} %reshape.305, f32[8,8,16,128]{3,2,1,0:T(8,128)S(1)} %bitcast.91, f32[64,2048]{1,0:T(8,128)S(1)} %reshape.304, f32[8,8,16,128]{3,2,1,0:T(8,128)S(1)} %bitcast.90, f32[64,2048]{1,0:T(8,128)S(1)} %reshape.298, f32[8,8,16,128]{3,2,1,0:T(8,128)S(1)} %bitcast.89), kind=kLoop, calls=%fused_computation.40 | loop fusion | flops 786432 | bytes 3407872 | tf_op jit(solution)/shard_map/convert_element_type | solution.py:199
  (81 shorter events, 1.7 us)
Async XLA Ops:
  0.0 22.7 %copy-start.1 = (bf16[1024,128]{1,0:T(8,128)(2,1)S(1)}, bf16[1024,128]{1,0:T(8,128)(2,1)}, u32[]{:S(2)}) copy-start(bf16[1024,128]{1,0:T(8,128)(2,1)} %param.12) | copy-start | bytes 786436
  0.0 22.7 %copy-start = (bf16[512,128]{1,0:T(8,128)(2,1)S(1)}, bf16[512,128]{1,0:T(8,128)(2,1)}, u32[]{:S(2)}) copy-start(bf16[512,128]{1,0:T(8,128)(2,1)} %param.14) | copy-start | bytes 393220
  0.0 22.7 %copy-start.7 = (f32[32,192]{1,0:T(8,128)S(1)}, f32[32,192]{1,0:T(8,128)}, u32[]{:S(2)}) copy-start(f32[32,192]{1,0:T(8,128)} %param.15) | copy-start | bytes 73732
  0.0 22.8 %copy-start.3 = (bf16[64,3072]{1,0:T(8,128)(2,1)S(1)}, bf16[64,3072]{1,0:T(8,128)(2,1)}, u32[]{:S(2)}) copy-start(bf16[64,3072]{1,0:T(8,128)(2,1)} %param.10) | copy-start | bytes 1179652
  0.0 23.4 %copy-start.8 = (f32[32,128]{1,0:T(8,128)S(1)}, f32[32,128]{1,0:T(8,128)}, u32[]{:S(2)}) copy-start(f32[32,128]{1,0:T(8,128)} %param.16) | copy-start | bytes 49156
  0.0 25.8 %copy-start.9 = (bf16[64,48]{0,1:T(8,128)(2,1)S(1)}, bf16[64,48]{0,1:T(8,128)(2,1)}, u32[]{:S(2)}) copy-start(bf16[64,48]{0,1:T(8,128)(2,1)} %param.17) | copy-start | bytes 18436
  3.0 38.8 %collective-permute-start = (bf16[16,192]{1,0:T(8,128)(2,1)}, bf16[16,192]{1,0:T(8,128)(2,1)}, u32[]{:S(2)}, u32[]{:S(2)}) collective-permute-start(bf16[16,192]{1,0:T(8,128)(2,1)} %get-tuple-element.13), channel_id=1, source_target_pairs={{0,24},{8,0},{16,8},{24,16},{1,25},{9,1},{17,9},{25,17},{2,26},{10... | collective-permute-start | bytes 18440 | tf_op jit(solution)/shard_map/ppermute | solution.py:18
  8.0 34.7 %collective-permute-start.1 = (bf16[16,192]{1,0:T(8,128)(2,1)}, bf16[16,192]{1,0:T(8,128)(2,1)}, u32[]{:S(2)}, u32[]{:S(2)}) collective-permute-start(bf16[16,192]{1,0:T(8,128)(2,1)} %get-tuple-element.14), channel_id=1, source_target_pairs={{0,24},{8,0},{16,8},{24,16},{1,25},{9,1},{17,9},{25,17},{2,26},{10... | collective-permute-start | bytes 18440 | tf_op jit(solution)/shard_map/ppermute | solution.py:18
  9.8 26.5 %collective-permute-start.2 = (bf16[16,128]{1,0:T(8,128)(2,1)}, bf16[16,128]{1,0:T(8,128)(2,1)}, u32[]{:S(2)}, u32[]{:S(2)}) collective-permute-start(bf16[16,128]{1,0:T(8,128)(2,1)} %get-tuple-element.15), channel_id=1, source_target_pairs={{0,24},{8,0},{16,8},{24,16},{1,25},{9,1},{17,9},{25,17},{2,26},{10... | collective-permute-start | bytes 12296 | tf_op jit(solution)/shard_map/ppermute | solution.py:18
  10.2 28.8 %collective-permute-start.3 = (bf16[16,128]{1,0:T(8,128)(2,1)}, bf16[16,128]{1,0:T(8,128)(2,1)}, u32[]{:S(2)}, u32[]{:S(2)}) collective-permute-start(bf16[16,128]{1,0:T(8,128)(2,1)} %get-tuple-element.16), channel_id=1, source_target_pairs={{0,24},{8,0},{16,8},{24,16},{1,25},{9,1},{17,9},{25,17},{2,26},{10... | collective-permute-start | bytes 12296 | tf_op jit(solution)/shard_map/ppermute | solution.py:18
  13.7 14.2 %all-to-all-start = ((s32[1,4,4]{1,0,2:T(1,128)}), s32[1,4,4]{1,0,2:T(1,128)S(1)}, u32[]{:S(2)}, u32[]{:S(2)}) async-start(s32[1,4,4]{1,0,2:T(1,128)} %copy.85), calls=%async_computation | async-start | bytes 4096 | tf_op jit(solution)/shard_map/all_to_all | solution.py:141
  19.9 48.9 %collective-permute-start.6 = (bf16[256,192]{0,1:T(8,128)(2,1)S(1)}, bf16[256,192]{0,1:T(8,128)(2,1)}, u32[]{:S(2)}, u32[]{:S(2)}) collective-permute-start(bf16[256,192]{0,1:T(8,128)(2,1)S(1)} %slice_select_fusion), channel_id=1, source_target_pairs={{0,8},{8,16},{16,24},{24,0},{1,9},{9,17},{17,25},{25,1},{2,10},{10... | collective-permute-start | bytes 294920 | tf_op jit(solution)/shard_map/ppermute | solution.py:18
  31.7 33.4 %all-to-all-start.2 = ((bf16[1,4,4,64,128]{4,3,1,0,2:T(8,128)(2,1)}), bf16[1,4,4,64,128]{4,3,1,0,2:T(8,128)(2,1)S(1)}, u32[]{:S(2)}, u32[]{:S(2)}) async-start(bf16[1,4,4,64,128]{4,3,1,0,2:T(8,128)(2,1)} %copy.95), calls=%async_computation.2 | async-start | bytes 524288 | tf_op jit(solution)/shard_map/all_to_all | solution.py:159
  36.3 34.7 %collective-permute-start.7 = (bf16[256,128]{1,0:T(8,128)(2,1)S(1)}, bf16[256,128]{1,0:T(8,128)(2,1)}, u32[]{:S(2)}, u32[]{:S(2)}) collective-permute-start(bf16[256,128]{1,0:T(8,128)(2,1)S(1)} %slice_select_fusion.1), channel_id=1, source_target_pairs={{0,8},{8,16},{16,24},{24,0},{1,9},{9,17},{17,25},{25,1},{2,10},{10... | collective-permute-start | bytes 196616 | tf_op jit(solution)/shard_map/ppermute | solution.py:18
  40.2 18.5 %collective-permute-start.4 = (bf16[96,128]{1,0:T(8,128)(2,1)S(1)}, bf16[96,128]{1,0:T(8,128)(2,1)S(1)}, u32[]{:S(2)}, u32[]{:S(2)}) collective-permute-start(bf16[96,128]{1,0:T(8,128)(2,1)S(1)} %pad_maximum_fusion.1), channel_id=1, source_target_pairs={{0,8},{8,0},{16,24},{24,16},{1,9},{9,1},{17,25},{25,17},{2,10},{10... | collective-permute-start | bytes 73736 | tf_op jit(solution)/shard_map/ppermute | solution.py:102
  43.5 14.4 %copy-start.11 = (s32[384]{0:T(512)S(1)}, s32[384]{0:T(512)}, u32[]{:S(2)}) copy-start(s32[384]{0:T(512)} %multiply_add_fusion) | copy-start | bytes 4612
  58.8 5.6 %collective-permute-start.5 = (bf16[192,128]{1,0:T(8,128)(2,1)S(1)}, bf16[192,128]{1,0:T(8,128)(2,1)S(1)}, u32[]{:S(2)}, u32[]{:S(2)}) collective-permute-start(bf16[192,128]{1,0:T(8,128)(2,1)S(1)} %maximum_select_fusion.2), channel_id=1, source_target_pairs={{0,16},{8,24},{16,0},{24,8},{1,17},{9,25},{17,1},{25,9},{2,18},{10... | collective-permute-start | bytes 147464 | tf_op jit(solution)/shard_map/ppermute | solution.py:102
  65.1 3.8 %copy-start.2 = (bf16[512,192]{0,1:T(8,128)(2,1)S(1)}, bf16[512,192]{0,1:T(8,128)(2,1)}, u32[]{:S(2)}) copy-start(bf16[512,192]{0,1:T(8,128)(2,1)} %param.13) | copy-start | bytes 589828
  65.1 3.8 %copy-start.10 = (s32[320]{0:T(512)S(1)}, s32[320]{0:T(512)}, u32[]{:S(2)}) copy-start(s32[320]{0:T(512)} %iota_add_fusion.1) | copy-start | bytes 3844
  65.2 13.7 %all-to-all-start.1 = ((bf16[1,4,4,64,192]{4,3,1,0,2:T(8,128)(2,1)}), bf16[1,4,4,64,192]{4,3,1,0,2:T(8,128)(2,1)S(1)}, u32[]{:S(2)}, u32[]{:S(2)}) async-start(bf16[1,4,4,64,192]{4,3,1,0,2:T(8,128)(2,1)} %copy_select_fusion), calls=%async_computation.1 | async-start | bytes 1048576 | tf_op jit(solution)/shard_map/all_to_all | solution.py:158
  72.4 6.5 %copy-start.12 = (pred[1024]{0:T(1024)(128)(4,1)S(1)}, pred[1024]{0:T(1024)(128)(4,1)}, u32[]{:S(2)}) copy-start(pred[1024]{0:T(1024)(128)(4,1)} %and.107) | copy-start | bytes 3076
  82.1 2.0 %copy-start.4 = (f32[64,16]{1,0:T(8,128)S(1)}, f32[64,16]{1,0:T(8,128)}, u32[]{:S(2)}) copy-start(f32[64,16]{1,0:T(8,128)} %copy.76) | copy-start | bytes 12292
  83.9 0.8 copy-start.5
  84.0 0.9 %copy-start.6 = (f32[64,16]{1,0:T(8,128)S(1)}, f32[64,16]{1,0:T(8,128)}, u32[]{:S(2)}) copy-start(f32[64,16]{1,0:T(8,128)} %copy.97) | copy-start | bytes 12292
